TPU v7x, 32 devices: a whole 2x2x4 slice. The times are simulated.
32 devices in a mesh: group: 2 (over x), dom: 16 (over z, y, core).
Axes of the slice: x: 2, y: 2, z: 4, core: 2. Of those that a mesh axis runs over, the one named last changes fastest.
Arguments:
- fields: float32 [6, 35, 32768], P(None, None, ('group', 'dom')), may hold values from -6 to 6
- metric: float32 [9, 32768], P(None, ('group', 'dom')), may hold values from -3 to 3
- face_scale: float32 [4, 32768], P(None, ('group', 'dom')), may hold values from 0.5 to 10
- face_angles: float32 [2, 4, 32768], P(None, None, ('group', 'dom')), may hold values from -3.140625 to 3.140625
- neighbours: int32 [4, 32768], P(None, ('group', 'dom')), may hold values from -1 to 4479, as said below
- send_dom: int32 [2, 4096], P(None, ('group', 'dom')), may hold values from 0 to 4095, as said below
- send_partner: int32 [4096], P(('group', 'dom')), may hold values from 0 to 4095, as said below
- element_kind: int32 [32768], P(('group', 'dom')), may hold values from 0 to 6, as said below
- derivative: float32 [3, 35, 35], replicated, may hold values from -1 to 1
- lifting: float32 [35, 60], replicated, may hold values from -0.75 to 0.75
- block_inverse: bfloat16 [6, 210, 210], replicated
Outputs:
- advanced: float32 [6, 35, 32768], P(None, None, ('group', 'dom'))
Inputs may be any that keep to these rules, and one draw needn't show every extreme that they name: `send_dom`: values are local face ids f * 1024 + e. Row 0 lists exactly the faces of the device whose neighbours slots are 4096 + i for i < 128, in the order of i; row 1 those with 4224 + i, in the order of i. `send_partner`: values are local face ids; exactly the faces of the device whose neighbours slot is 4352 + i, in the order of i. `neighbours`: on each device: every slot from 4096 up is read by exactly one face; 128 faces hold -1; every other face holds the id of another face of the same device, and that face holds its id. `element_kind`: elements of kind 1 or more (the fine region) lie exactly on the devices with group index 1 and dom index at least half of the dom axis; all elements of those devices have kind 1 or more, all others kind 0.
All inputs are finite; a program needn't handle non-finite values.
Results may differ from a plain program's by a relative error of at most 0.0003.
Values sent between devices are 32-bit elements; how exact they have to be, the bound alone decides.
A program may use at most 64 MiB of HBM per device.

v0:
```python
import functools

import jax
import jax.numpy as jnp
import numpy as np
from jax import lax
from jax.experimental import pallas as pl
from jax.experimental.pallas import tpu as pltpu
from jax.sharding import PartitionSpec as P

SWEEPS = 4
STEP = 0.2
NC, NP, NFP = 6, 35, 15
RP = 40
KP = 48
FP = 16
CHUNK = 512
SUB = 128
f32, bf16 = jnp.float32, jnp.bfloat16


def face_nodes():
    lattice = [(r, s, t) for r in range(5) for s in range(5 - r) for t in range(5 - r - s)]
    tests = [
        lambda p: p[2] == 0,
        lambda p: p[1] == 0,
        lambda p: p[0] == 0,
        lambda p: sum(p) == 4,
    ]
    return [[i for i, p in enumerate(lattice) if test(p)] for test in tests]


def constants():
    trace = np.zeros((4 * FP, NP), np.float32)
    for f, nodes in enumerate(face_nodes()):
        for n, node in enumerate(nodes):
            trace[f * FP + n, node] = 1
    trace3 = np.zeros((4 * FP, 3 * KP), np.float32)
    trace3[:, :NP] = trace
    trace3[:, 2 * KP : 2 * KP + NP] = trace
    spread = np.zeros((2, NP, 3 * KP), np.float32)
    for i in range(NP):
        spread[0, i, i] = spread[0, i, 2 * KP + i] = spread[1, i, KP + i] = 1
    lift_spread = np.zeros((2, 4 * NFP, 3 * 4 * FP), np.float32)
    for f in range(4):
        for n in range(NFP):
            row, col = f * NFP + n, f * FP + n
            lift_spread[0, row, col] = lift_spread[0, row, 8 * FP + col] = 1
            lift_spread[1, row, 4 * FP + col] = 1
    trace6 = np.kron(np.eye(NC, dtype=np.float32), trace)
    rows6 = np.kron(np.eye(NC, dtype=np.float32), np.eye(RP, NP, dtype=np.float32))
    cols6 = np.concatenate([rows6.T, rows6.T], axis=1)
    return [jnp.asarray(a, bf16) for a in (trace3, spread, lift_spread, trace6, rows6, cols6)]


def split(x):
    hi = x.astype(bf16)
    return hi, (x - hi.astype(f32)).astype(bf16)


def dot(a, b):
    return jnp.dot(a, b, preferred_element_type=f32)


def kernel(
    el, fields, metric, scale, angles, nb, send_dom, send_part, kind, deriv, lift, binv,
    trace3, spread, lift_spread, trace6, rows6, cols6,
    out,
    fpad, d3, l3, wt, wf, grads, tr, own, recv_n, coef, sel, sel_send, pool, remote, ext, rhs,
    base, sendbuf, recvbuf, send_sem, recv_sem,
):
    grp, dom = lax.axis_index("group"), lax.axis_index("dom")
    count = lax.axis_size("dom")
    half = count // 2
    fine = jnp.logical_and(grp == 1, dom >= half)
    halves = el // CHUNK
    chunks = 4 * halves
    has_prev, has_next = dom > 0, dom < count - 1
    fine_prev = jnp.logical_and(fine, dom > half)
    fine_next = jnp.logical_and(fine, has_next)

    barrier = pltpu.get_barrier_semaphore()

    @pl.when(has_prev)
    def _():
        pl.semaphore_signal(barrier, inc=1, device_id={"dom": dom - 1})

    @pl.when(has_next)
    def _():
        pl.semaphore_signal(barrier, inc=1, device_id={"dom": dom + 1})

    pl.semaphore_signal(barrier, inc=1, device_id={"group": 1 - grp})

    def slot(f):
        row = nb[f : f + 1, :]
        lane = lax.broadcasted_iota(jnp.int32, (1, el), 1)
        return jnp.where(row < 0, lane + f * el, row)

    def send_list():
        return jnp.concatenate([send_dom[0:1, :], send_dom[1:2, :], send_part[...]], axis=1)

    def pair_copies(step):
        targets = ({"dom": dom - 1}, {"dom": dom + 1}, {"group": 1 - grp})
        lands = (1, 0, 2)
        return [
            pltpu.make_async_remote_copy(
                src_ref=sendbuf.at[step, i],
                dst_ref=recvbuf.at[step, lands[i]],
                send_sem=send_sem.at[step, i],
                recv_sem=recv_sem.at[step, lands[i]],
                device_id=targets[i],
            )
            for i in range(3)
        ]

    def start(step, to_prev, to_next, partner):
        copies = pair_copies(step)

        @pl.when(to_prev)
        def _():
            copies[0].start()

        @pl.when(to_next)
        def _():
            copies[1].start()

        if partner:
            copies[2].start()

    def finish(step, from_prev, from_next, partner):
        copies = pair_copies(step)

        @pl.when(from_prev)
        def _():
            copies[0].wait_send()
            copies[1].wait_recv()
            remote[0] = recvbuf[step, 0]

        @pl.when(from_next)
        def _():
            copies[1].wait_send()
            copies[0].wait_recv()
            remote[1] = recvbuf[step, 1]

        if partner:
            copies[2].wait()
            remote[2] = recvbuf[step, 2]

    def pool_store(f, x):
        rows = x.shape[0]
        hi = x.astype(bf16).astype(f32)
        both = jnp.concatenate([hi, x - hi], axis=0).astype(bf16)
        for k in range(halves):
            h = f * halves + k
            pool[h * 2 * rows : (h + 1) * 2 * rows, :] = both[:, k * CHUNK : (k + 1) * CHUNK]

    def pick(y, which, rows, total=None):
        if total is None:
            total = jnp.zeros((rows, y.shape[1]), f32)
        for h in range(chunks):
            at = h * 2 * rows
            value = y[at : at + rows] + y[at + rows : at + 2 * rows]
            total = jnp.where(which == h, value, total)
        return total

    def outgoing(step, rows, lists=3):
        y = dot(pool[: chunks * 2 * rows, :], sel_send[:, : lists * SUB])
        picked = pick(y, (send_list() // CHUNK)[:, : lists * SUB], rows)
        for i in range(lists):
            sendbuf[step, i, 0:rows, :] = picked[:, i * SUB : (i + 1) * SUB]

    def gather_local(rows, dest, start_from=None):
        for f in range(4):
            y = dot(pool[: chunks * 2 * rows, :], sel[:, f * el : (f + 1) * el])
            under = None if start_from is None else start_from[f]
            dest[f] = pick(y, slot(f) // CHUNK, rows, under)

    def gather_remote(rows, dest, lists=3):
        x = jnp.concatenate([remote[i, 0:rows, :] for i in range(lists)], axis=1)
        hi = x.astype(bf16).astype(f32)
        both = jnp.concatenate([hi, x - hi], axis=0).astype(bf16)
        for f in range(4):
            y = dot(both, sel[0 : lists * SUB, f * el : (f + 1) * el])
            here = slot(f)
            there = jnp.logical_and(here >= 4 * el, here < 4 * el + lists * SUB)
            dest[f] = jnp.where(there, y[:rows] + y[rows:], dest[f])

    polar, azimuth = angles[0], angles[1]
    parts = (jnp.sin(polar), jnp.cos(polar), jnp.sin(azimuth), jnp.cos(azimuth))
    own[...] = jnp.zeros_like(own)
    for f in range(4):
        for i in range(4):
            own[f, i : i + 1, :] = parts[i][f : f + 1, :]
        w = 0.5 * scale[f : f + 1, :]
        sa, ca, sb, cb = (p[f : f + 1, :] for p in parts)
        for i, row in enumerate((w * ca * cb, w * ca * sb, -w * sa, -w * sb, w * cb)):
            coef[f, i : i + 1, :] = row
        pool_store(f, own[f])
    down = lax.broadcasted_iota(jnp.int32, (CHUNK, 3 * SUB), 0)
    sel_send[...] = jnp.where(down == send_list() % CHUNK, 1.0, 0.0).astype(bf16)
    remote[...] = jnp.zeros_like(remote)
    sendbuf[0] = jnp.zeros_like(sendbuf[0])

    outgoing(0, 8)
    pl.semaphore_wait(
        barrier, 1 + has_prev.astype(jnp.int32) + has_next.astype(jnp.int32)
    )
    start(0, has_prev, has_next, True)

    for f in range(4):
        down = lax.broadcasted_iota(jnp.int32, (CHUNK, el), 0)
        sel[:, f * el : (f + 1) * el] = jnp.where(down == slot(f) % CHUNK, 1.0, 0.0).astype(bf16)
    gather_local(8, recv_n)

    fpad[...] = jnp.zeros_like(fpad)
    d3[...] = jnp.zeros_like(d3)
    l3[...] = jnp.zeros_like(l3)
    for b in range(3):
        hi, lo = split(deriv[b])
        d3[b * RP : b * RP + NP, :] = dot(hi, spread[0]) + dot(lo, spread[1])
    d3[3 * RP : 3 * RP + 4 * FP, :] = trace3[...].astype(f32)
    hi, lo = split(lift[...])
    l3[0:NP, :] = dot(hi, lift_spread[0]) + dot(lo, lift_spread[1])
    d3b = d3[...].astype(bf16)
    for c in range(NC):
        fpad[c, 0:NP, :] = fields[c]
        hi, lo = split(fpad[c])
        y = dot(d3b, jnp.concatenate([hi, hi, lo], axis=0))
        grads[c] = y[: 3 * RP]
        tr[c * 4 * FP : (c + 1) * 4 * FP, :] = y[3 * RP :]

    def trace_pq(f, n_ref, sign):
        at = [tr[c * 4 * FP + f * FP : c * 4 * FP + (f + 1) * FP, :] for c in range(NC)]
        sa, ca, sb, cb = (n_ref[f, i : i + 1, :] for i in range(4))
        if sign is not None:
            at[:3] = [sign * e for e in at[:3]]
        e_t = ca * (cb * at[0] + sb * at[1]) - sa * at[2]
        e_p = cb * at[1] - sb * at[0]
        h_t = ca * (cb * at[3] + sb * at[4]) - sa * at[5]
        h_p = cb * at[4] - sb * at[3]
        return jnp.concatenate([h_p - e_t, -h_t - e_p], axis=0)

    def fill_pool():
        for f in range(4):
            sign = jnp.where(nb[f : f + 1, :] < 0, -1.0, 1.0)
            pool_store(f, trace_pq(f, recv_n, sign))

    def lifted(pq):
        for c in range(NC):
            rows = []
            for f in range(4):
                p, q = pq[f][:FP], pq[f][FP:]
                a, b = (p, q) if c < 3 else (q, -p)
                k = c % 3
                row = coef[f, k : k + 1, :] * a
                if k < 2:
                    row = row + coef[f, 3 + k : 4 + k, :] * b
                rows.append(row)
            hi, lo = split(jnp.concatenate(rows, axis=0))
            yield c, dot(l3[...].astype(bf16), jnp.concatenate([hi, hi, lo], axis=0))

    finish(0, has_prev, has_next, True)
    gather_remote(8, recv_n)
    fill_pool()
    outgoing(1, 2 * FP)
    start(1, has_prev, has_next, True)
    gather_local(2 * FP, ext)

    @pl.when(fine)
    def _():
        for k in range(binv.shape[0]):
            b2 = dot(binv[k], cols6[...]).astype(bf16)
            wt[k] = dot(trace6[...], b2).astype(bf16)
            wf[k] = dot(rows6[...], b2).astype(bf16)

    remote[...] = jnp.zeros_like(remote)
    finish(1, has_prev, has_next, True)
    gather_remote(2 * FP, ext)

    @pl.when(jnp.logical_not(fine))
    def _():
        pq = [trace_pq(f, own, None) - ext[f] for f in range(4)]

        def along(c, axis):
            return sum(
                metric[3 * axis + b : 3 * axis + b + 1, :] * grads[c, b * RP : (b + 1) * RP, :]
                for b in range(3)
            )

        for c, s in lifted(pq):
            k, other = c % 3, 3 - 3 * (c // 3)
            one, two = (k + 1) % 3, (k + 2) % 3
            curl = along(other + two, one) - along(other + one, two)
            vol = curl if c < 3 else -curl
            out[c] = (fpad[c, 0:RP, :] + STEP * (vol + s))[:NP]

    @pl.when(fine)
    def _():
        def right_side():
            terms = [
                fpad[c, 0:RP, :] - STEP * s for c, s in lifted([ext[f] for f in range(4)])
            ]
            hi, lo = split(jnp.concatenate(terms, axis=0))
            rhs[0 : NC * RP, :] = hi
            rhs[NC * RP : 2 * NC * RP, :] = lo

        def blocks(weights, k):
            mask = jnp.where(kind[...] == k + 1, 1.0, 0.0).astype(bf16)
            return dot(weights[k], rhs[...] * mask)

        for f in range(4):
            base[f] = jnp.where(slot(f) >= 4 * el + 2 * SUB, ext[f], 0.0)

        def sweep(no, carry):
            right_side()
            tr[...] = blocks(wt, 0)
            for k in range(1, binv.shape[0]):
                tr[...] += blocks(wt, k)
            fill_pool()
            outgoing(no, 2 * FP, 2)
            start(no, fine_prev, fine_next, False)
            gather_local(2 * FP, ext, base)
            finish(no, fine_prev, fine_next, False)
            gather_remote(2 * FP, ext, 2)
            return carry

        lax.fori_loop(2, SWEEPS + 1, sweep, 0)
        right_side()
        total = blocks(wf, 0)
        for k in range(1, binv.shape[0]):
            total += blocks(wf, k)
        for c in range(NC):
            out[c] = total[c * RP : c * RP + NP]


def shards(*args):
    (fields, metric, scale, angles, nb, send_dom, send_part, kind, deriv, lift, binv) = args
    el = fields.shape[2]
    kinds = binv.shape[0]
    operands = [
        fields, metric, scale, angles, nb, send_dom, send_part.reshape(1, -1),
        kind.reshape(1, -1), deriv, lift, binv, *constants(),
    ]
    vmem = pltpu.VMEM
    return pl.pallas_call(
        functools.partial(kernel, el),
        out_shape=jax.ShapeDtypeStruct(fields.shape, f32),
        in_specs=[pl.BlockSpec(memory_space=vmem)] * len(operands),
        out_specs=pl.BlockSpec(memory_space=vmem),
        scratch_shapes=[
            vmem((NC, KP, el), f32),
            vmem((3 * RP + 4 * FP, 3 * KP), f32),
            vmem((RP, 12 * FP), f32),
            vmem((kinds, NC * 4 * FP, 2 * NC * RP), bf16),
            vmem((kinds, NC * RP, 2 * NC * RP), bf16),
            vmem((NC, 3 * RP, el), f32),
            vmem((NC * 4 * FP, el), f32),
            vmem((4, 8, el), f32),
            vmem((4, 8, el), f32),
            vmem((4, 8, el), f32),
            vmem((CHUNK, 4 * el), bf16),
            vmem((CHUNK, 3 * SUB), bf16),
            vmem((4 * (el // CHUNK) * 4 * FP, CHUNK), bf16),
            vmem((3, 2 * FP, SUB), f32),
            vmem((4, 2 * FP, el), f32),
            vmem((2 * NC * RP, el), bf16),
            vmem((4, 2 * FP, el), f32),
            vmem((SWEEPS + 1, 3, 2 * FP, SUB), f32),
            vmem((SWEEPS + 1, 3, 2 * FP, SUB), f32),
            pltpu.SemaphoreType.DMA((SWEEPS + 1, 3)),
            pltpu.SemaphoreType.DMA((SWEEPS + 1, 3)),
        ],
        compiler_params=pltpu.CompilerParams(
            collective_id=0, has_side_effects=True, vmem_limit_bytes=56 * 2**20
        ),
    )(*operands)


def solution(mesh):
    both = ("group", "dom")
    in_specs = (
        P(None, None, both), P(None, both), P(None, both), P(None, None, both), P(None, both),
        P(None, both), P(both), P(both), P(), P(), P(),
    )
    return jax.shard_map(
        shards, mesh=mesh, in_specs=in_specs, out_specs=P(None, None, both), check_vma=False
    )
```

profile of v0, /device:TPU:23, one launch (start us, length us, event | category | flops | bytes accessed | tf_op | source)
XLA Modules:
  0.0 39.6 jit_solution(3715111580375423761)
XLA Ops:
  0.0 37.3 %shard_map.163 = f32[6,35,1024]{2,1,0:T(8,128)} custom-call(f32[6,35,1024]{2,1,0:T(8,128)} %fields.1, f32[9,1024]{1,0:T(8,128)} %metric.1, f32[4,1024]{1,0:T(4,128)} %scale.1, f32[2,4,1024]{2,1,0:T(4,128)} %angles.1, s32[4,1024]{1,0:T(4,128)} %nb.1, s32[2,128]{1,0:T(2,128)} %send_dom.1, s32[1,128]{1,0:T(1,128)} %bitcast.3, s32[1,1024]{1,0:T(1,128)} %bitcast.2, ...), custom_call_target="tpu_custom_call" | custom-call | tf_op jit(solution)/shard_map/pallas_call | solution.py:345
  37.4 2.2 %copy.19 = f32[6,35,1024]{2,1,0:T(8,128)} copy(f32[6,35,1024]{2,1,0:T(8,128)} %shard_map.163) | data formatting | bytes 1720320
where the time goes:
time: 39.8 us; the launch traced here: 39.6 us
  Pallas kernels  37.3 us (94%)
  local copies, waits for them, and re-layouts  2.25 us (6%)
    pallas_call x1, Pallas kernels, shards(): pl.pallas_call(functools.partial(kernel, el), out_shape=jax.ShapeDtypeStr...  37.3 us
    unnamed x1, local copies, waits for them, and re-layouts  2.25 us

commit v1 on v0

v1 whole, which is shorter than its diff:
```python
import functools

import jax
import jax.numpy as jnp
import numpy as np
from jax import lax
from jax.experimental import pallas as pl
from jax.experimental.pallas import tpu as pltpu
from jax.sharding import PartitionSpec as P

SWEEPS = 4
STEP = 0.2
NC, NP, NFP = 6, 35, 15
RP = 40
HB = NC * RP
KB = 256
FP = 16
TR = NC * 4 * FP
TILE = 256
SUB = 128
MSG = NC * FP + 8
f32, bf16, i32 = jnp.float32, jnp.bfloat16, jnp.int32


def face_nodes():
    lattice = [(r, s, t) for r in range(5) for s in range(5 - r) for t in range(5 - r - s)]
    tests = [
        lambda p: p[2] == 0,
        lambda p: p[1] == 0,
        lambda p: p[0] == 0,
        lambda p: sum(p) == 4,
    ]
    return [[i for i, p in enumerate(lattice) if test(p)] for test in tests]


def constants(el, kinds):
    trace = np.zeros((4 * FP, NP), np.float32)
    for f, nodes in enumerate(face_nodes()):
        for n, node in enumerate(nodes):
            trace[f * FP + n, node] = 1
    eye6 = np.eye(NC, dtype=np.float32)
    pad = np.eye(RP, NP, dtype=np.float32)
    trace6 = np.kron(eye6, trace)
    rows6 = np.kron(eye6, pad)
    cols6 = np.zeros((NC * NP, KB), np.float32)
    cols6[:, :HB] = rows6.T
    tracep = np.tile(trace6 @ cols6, (1, 2))
    spread = np.zeros((2, NP, 3 * RP), np.float32)
    for i in range(NP):
        spread[0, i, i] = spread[0, i, RP + i] = spread[1, i, 2 * RP + i] = 1
    lift_spread = np.zeros((4, 4 * NFP, 16 * FP), np.float32)
    for f in range(4):
        for n in range(NFP):
            row, col = f * NFP + n, f * FP + n
            for i in range(2):
                lift_spread[2 * i, row, 8 * FP * i + col] = 1
                lift_spread[2 * i, row, 8 * FP * i + 4 * FP + col] = 1
                lift_spread[2 * i + 1, row, 8 * FP * i + col] = 1
    upper = np.concatenate([np.triu(np.ones((SUB, SUB)), 1), np.ones((SUB, SUB))], axis=1)
    lines = (kinds + 1) * (el // SUB)
    lower = np.tril(np.ones((lines, lines)), -1)
    small = [jnp.asarray(a, bf16) for a in (upper, lower, spread, lift_spread)]
    large = [jnp.asarray(a, bf16) for a in (tracep, trace6, rows6, cols6)]
    return small, large


def split(x):
    hi = x.astype(bf16)
    return hi, (x - hi.astype(f32)).astype(bf16)


def dot(a, b):
    return jnp.dot(a, b, preferred_element_type=f32)


def stacked(x):
    hi, lo = split(x)
    gap = jnp.zeros((KB - HB, x.shape[1]), bf16)
    return jnp.concatenate([hi, gap, lo, gap], axis=0)


def project(at, n):
    sa, ca, sb, cb = n
    e_t = ca * (cb * at[0] + sb * at[1]) - sa * at[2]
    e_p = cb * at[1] - sb * at[0]
    h_t = ca * (cb * at[3] + sb * at[4]) - sa * at[5]
    h_p = cb * at[4] - sb * at[3]
    return jnp.concatenate([h_p - e_t, -h_t - e_p], axis=0)


def lanes(x, index):
    return jnp.take_along_axis(x, jnp.broadcast_to(index, x.shape), axis=1)


def kernel(
    el, kinds, scale, angles, nb, send_dom, send_part, kind, deriv, lift,
    upper, lower, spread, lift_spread,
    fields_h, metric_h, binv_h, tracep_h, trace6_h, rows6_h, cols6_h,
    out,
    fraw, metric, binv, tracep, trace6, rows6, cols6,
    fpad, own, xs, ohs, lnorm, slots, sgn, kindrow, offs, lsl, pm, sel, pooln, pool, recvn, coef,
    d3, l2, trs, ext, base, rem, remn, wt, wf, rhs, zs, pq0, grads,
    send0, recv0, sendk, recvk, off, walk,
    in_sem, ssem0, rsem0, ssemk, rsemk,
):
    grp, dom = lax.axis_index("group"), lax.axis_index("dom")
    count = lax.axis_size("dom")
    half = count // 2
    fine = jnp.logical_and(grp == 1, dom >= half)
    coarse = jnp.logical_not(fine)
    nt = el // TILE
    shift = el.bit_length() - 1
    lines = el // SUB
    steps = nt - 1 + kinds - 1
    has_prev, has_next = dom > 0, dom < count - 1
    fine_prev = jnp.logical_and(fine, dom > half)
    fine_next = jnp.logical_and(fine, has_next)

    loads = [
        pltpu.make_async_copy(a, b, in_sem.at[i])
        for i, (a, b) in enumerate((
            (fields_h, fraw), (tracep_h, tracep), (cols6_h, cols6), (binv_h, binv),
            (trace6_h, trace6), (rows6_h, rows6), (metric_h, metric),
        ))
    ]
    for load in loads:
        load.start()

    barrier = pltpu.get_barrier_semaphore()

    @pl.when(has_prev)
    def _():
        pl.semaphore_signal(barrier, inc=1, device_id={"dom": dom - 1})

    @pl.when(has_next)
    def _():
        pl.semaphore_signal(barrier, inc=1, device_id={"dom": dom + 1})

    pl.semaphore_signal(barrier, inc=1, device_id={"group": 1 - grp})

    targets = ({"dom": dom - 1}, {"dom": dom + 1}, {"group": 1 - grp})
    lands = (1, 0, 2)
    first = [
        pltpu.make_async_remote_copy(
            src_ref=send0.at[i], dst_ref=recv0.at[lands[i]],
            send_sem=ssem0.at[i], recv_sem=rsem0.at[lands[i]], device_id=targets[i],
        )
        for i in range(3)
    ]

    def later(no):
        return [
            pltpu.make_async_remote_copy(
                src_ref=sendk.at[no - 1, i], dst_ref=recvk.at[no - 1, lands[i]],
                send_sem=ssemk.at[no - 1, i], recv_sem=rsemk.at[no - 1, lands[i]],
                device_id=targets[i],
            )
            for i in range(2)
        ]

    polar, azimuth = angles[0], angles[1]
    parts = (jnp.sin(polar), jnp.cos(polar), jnp.sin(azimuth), jnp.cos(azimuth))
    own[...] = jnp.zeros_like(own)
    for f in range(4):
        for i in range(4):
            own[f * 8 + i : f * 8 + i + 1, :] = parts[i][f : f + 1, :]
        own[f * 8 + 4 : f * 8 + 5, :] = 0.5 * scale[f : f + 1, :]
    lists = jnp.concatenate([send_dom[0:1, :], send_dom[1:2, :], send_part[...]], axis=1)
    down = lax.broadcasted_iota(i32, (el, 3 * SUB), 0)
    ohs[...] = jnp.where(down == (lists & (el - 1)), 1.0, 0.0).astype(bf16)
    xs[2 * HB : 2 * HB + 32, :], xs[2 * HB + 32 : 2 * HB + 64, :] = split(own[...])

    loads[0].wait()
    for c in range(NC):
        fpad[c * RP + 32 : (c + 1) * RP, :] = jnp.zeros((8, el), f32)
        fpad[c * RP : c * RP + NP, :] = fraw[c]
    xs[0:HB, :], xs[HB : 2 * HB, :] = split(fpad[...])
    loads[1].wait()
    y = dot(xs[...], ohs[...])
    at_list = y[2 * HB : 2 * HB + 32] + y[2 * HB + 32 : 2 * HB + 64]
    face = lists >> shift
    mine = at_list[0:8]
    for f in range(1, 4):
        mine = jnp.where(face == f, at_list[f * 8 : (f + 1) * 8], mine)
    lnorm[...] = mine
    t = dot(tracep[...], stacked(y[0:HB] + y[HB : 2 * HB]))
    for c in range(NC):
        v = t[c * 4 * FP : c * 4 * FP + FP]
        for f in range(1, 4):
            v = jnp.where(face == f, t[(c * 4 + f) * FP : (c * 4 + f + 1) * FP], v)
        for i in range(3):
            send0[i, c * FP : (c + 1) * FP, :] = v[:, i * SUB : (i + 1) * SUB]
    for i in range(3):
        send0[i, NC * FP : MSG, :] = mine[:, i * SUB : (i + 1) * SUB]

    pl.semaphore_wait(barrier, 1 + has_prev.astype(i32) + has_next.astype(i32))

    @pl.when(has_prev)
    def _():
        first[0].start()

    @pl.when(has_next)
    def _():
        first[1].start()

    first[2].start()

    @pl.when(coarse)
    def _():
        for f in range(4):
            row = nb[f : f + 1, :]
            lane = lax.broadcasted_iota(i32, (1, el), 1)
            slots[f : f + 1, :] = jnp.where(row < 0, lane + f * el, row)
            sgn[f : f + 1, :] = jnp.where(row < 0, -1.0, 1.0)

    @pl.when(fine)
    def _():
        def square(row):
            return jnp.concatenate([row[:, i * SUB : (i + 1) * SUB] for i in range(lines)], axis=0)

        def line(sq):
            return jnp.concatenate([sq[i : i + 1] for i in range(lines)], axis=1)

        faces = [square(nb[f : f + 1, :]) for f in range(4)]
        which = square(kind[...])
        edge = functools.reduce(
            jnp.logical_or,
            [jnp.logical_and(n >= 4 * el, n < 4 * el + 2 * SUB) for n in faces],
        )
        group = jnp.where(edge, 0, which)
        masks = jnp.concatenate(
            [jnp.where(group == k, 1.0, 0.0) for k in range(kinds + 1)], axis=0
        )
        pre = dot(masks.astype(bf16), upper[...])
        before = dot(lower[...], pre[:, SUB:].astype(bf16))
        ranks = masks * (pre[:, :SUB] + before)
        pos = sum(ranks[k * lines : (k + 1) * lines] for k in range(kinds + 1))
        offs[...] = before.astype(i32)
        for k in range(kinds):
            off[k] = offs[(k + 1) * lines, 0]
        off[kinds] = jnp.int32(el)
        t, k = jnp.int32(1), jnp.int32(1)
        seen = [jnp.int32(-1)] * nt
        for s in range(steps):
            lo, hi = off[k - 1], off[k]
            walk[0, s] = t
            walk[1, s] = k - 1
            walk[2, s] = lo - t * TILE
            walk[3, s] = hi - t * TILE
            seen = [n + jnp.where(t <= i, 1, 0) for i, n in enumerate(seen)]
            stay = jnp.logical_and(hi <= (t + 1) * TILE, k < kinds)
            k, t = jnp.where(stay, k + 1, k), jnp.where(stay, t, jnp.minimum(t + 1, nt - 1))
        for i in range(nt):
            walk[4, i] = jnp.clip(seen[i], 0, steps - 1)

        def lookup(e):
            lane, row = e & (SUB - 1), e >> (SUB.bit_length() - 1)
            res = jnp.zeros((lines, SUB), f32)
            for r in range(lines):
                table = jnp.broadcast_to(pos[r : r + 1], (lines, SUB))
                res = jnp.where(row == r, jnp.take_along_axis(table, lane, axis=1), res)
            return res.astype(i32)

        place = pos.astype(i32)
        for f in range(4):
            n = faces[f]
            inner = (n >> shift) * el + lookup(n & (el - 1))
            m = jnp.where(n < 0, f * el + place, jnp.where(n >= 4 * el, n, inner))
            flag = 2 * which + jnp.where(n < 0, 1, 0)
            for i, v in enumerate((m >> 6, m & 63, flag)):
                own[f * 8 + 5 + i : f * 8 + 6 + i, :] = line(v.astype(f32))
        mine = jnp.concatenate([send_dom[...]] * (lines // 2), axis=0)
        lsl[...] = (mine >> shift) * TILE + lookup(mine & (el - 1))

        row = line(place)
        for i in range(nt):
            down = lax.broadcasted_iota(i32, (TILE, el), 0) + i * TILE
            pm[i * TILE : (i + 1) * TILE, :] = jnp.where(down == row, 1.0, 0.0).astype(bf16)
        xs[2 * HB : 2 * HB + 32, :], xs[2 * HB + 32 : 2 * HB + 64, :] = split(own[...])
        y = lax.dot_general(
            xs[...], pm[...], (((1,), (1,)), ((), ())), preferred_element_type=f32
        )
        fpad[...] = y[0:HB] + y[HB : 2 * HB]
        own[...] = y[2 * HB : 2 * HB + 32] + y[2 * HB + 32 : 2 * HB + 64]
        for f in range(4):
            at = f * 8 + 5
            slots[f : f + 1, :] = (own[at : at + 1, :] * 64 + own[at + 1 : at + 2, :]).astype(i32)
            flag = own[at + 2 : at + 3, :].astype(i32)
            sgn[f : f + 1, :] = jnp.where((flag & 1) == 1, -1.0, 1.0)
            if f == 0:
                kindrow[...] = flag >> 1

    def pick(y, f, rows, total):
        which = slots[f : f + 1, :] >> (TILE.bit_length() - 1)
        for h in range(4 * nt):
            total = jnp.where(which == h, y[h * rows : (h + 1) * rows], total)
        return total

    def gather(source, rows, dest, under=None):
        for f in range(4):
            s = sel[:, f * el : (f + 1) * el]
            y = dot(source[...], jnp.concatenate([s, s], axis=0))
            dest[f] = pick(y, f, rows, jnp.zeros((rows, el), f32) if under is None else under[f])

    def place_at(dest, source, f, j, sources):
        s = slots[f : f + 1, j * SUB : (j + 1) * SUB]
        v = dest[f, :, j * SUB : (j + 1) * SUB]
        for i in sources:
            here = (s >> (SUB.bit_length() - 1)) == 4 * el // SUB + i
            v = jnp.where(here, lanes(source[i], s & (SUB - 1)), v)
        dest[f, :, j * SUB : (j + 1) * SUB] = v

    def fill(t, at_rows):
        cols = slice(t * TILE, (t + 1) * TILE)
        for f in range(4):
            at = [at_rows(c * 4 * FP + f * FP) for c in range(NC)]
            sign = sgn[f : f + 1, cols]
            at[:3] = [sign * e for e in at[:3]]
            pq = project(at, [recvn[f, i : i + 1, cols] for i in range(4)])
            hi, lo = split(pq)
            h = f * nt + t
            pool[h * 2 * FP : (h + 1) * 2 * FP, 0:TILE] = hi
            pool[h * 2 * FP : (h + 1) * 2 * FP, TILE : 2 * TILE] = lo
            if t == 0:
                pq0[f] = pq

    down = lax.broadcasted_iota(i32, (TILE, el), 0)
    for f in range(4):
        low = slots[f : f + 1, :] & (TILE - 1)
        sel[:, f * el : (f + 1) * el] = jnp.where(down == low, 1.0, 0.0).astype(bf16)
    for f in range(4):
        for t in range(0, nt, 2):
            both = [own[f * 8 : f * 8 + 8, (t + i) * TILE : (t + i + 1) * TILE] for i in range(2)]
            h = (f * nt + t) * 8
            pooln[h : h + 16, 0:TILE], pooln[h : h + 16, TILE : 2 * TILE] = split(
                jnp.concatenate(both, axis=0)
            )
        sa, ca, sb, cb, w = (own[f * 8 + i : f * 8 + i + 1, :] for i in range(5))
        for i, row in enumerate((w * ca * cb, w * ca * sb, -w * sa, -w * sb, w * cb)):
            coef[f, i : i + 1, :] = row
    gather(pooln, 8, recvn)
    for t in range(nt):
        z = dot(tracep[...], stacked(fpad[:, t * TILE : (t + 1) * TILE]))
        trs[t] = z
        fill(t, lambda r: z[r : r + FP])
    gather(pool, 2 * FP, ext)

    l2[...] = jnp.zeros_like(l2)
    hi, lo = split(lift[...])
    for i in range(4):
        l2[i * RP : i * RP + NP, :] = dot(lo if i % 2 else hi, lift_spread[i])
    for load in loads[2:]:
        load.wait()

    @pl.when(fine)
    def _():
        for k in range(kinds):
            b2 = dot(binv[k], cols6[...]).astype(bf16)
            a = dot(trace6[...], b2).astype(bf16)
            b = dot(rows6[...], b2).astype(bf16)
            for i in range(2):
                wt[k, :, i * KB : (i + 1) * KB] = a
                wf[k, :, i * KB : (i + 1) * KB] = b

    @pl.when(coarse)
    def _():
        d3[...] = jnp.zeros_like(d3)
        for b in range(3):
            hi, lo = split(deriv[b])
            d3[b * RP : b * RP + NP, :] = dot(hi, spread[0]) + dot(lo, spread[1])
        db = d3[...].astype(bf16)
        for c in range(NC):
            x = fpad[c * RP : (c + 1) * RP, :]
            hi = x.astype(bf16).astype(f32)
            grads[c] = dot(db, jnp.concatenate([hi, x - hi, hi], axis=0).astype(bf16))

    def arrive(i):
        at = [recv0[i, c * FP : (c + 1) * FP, :] for c in range(NC)]
        rem[i] = project(at, [lnorm[r : r + 1, i * SUB : (i + 1) * SUB] for r in range(4)])
        remn[i] = recv0[i, NC * FP : MSG, :]

    rem[...] = jnp.zeros_like(rem)
    remn[...] = jnp.zeros_like(remn)

    @pl.when(has_prev)
    def _():
        first[0].wait_send()
        first[1].wait_recv()
        arrive(0)

    @pl.when(has_next)
    def _():
        first[1].wait_send()
        first[0].wait_recv()
        arrive(1)

    first[2].wait()
    arrive(2)

    def lifted(t, pq):
        cols = slice(t * TILE, (t + 1) * TILE)
        for pair in range(NC // 2):
            pieces = []
            for c in (2 * pair, 2 * pair + 1):
                rows = []
                k = c % 3
                for f in range(4):
                    p, q = pq[f][:FP], pq[f][FP:]
                    a, b = (p, q) if c < 3 else (q, -p)
                    row = coef[f, k : k + 1, cols] * a
                    if k < 2:
                        row = row + coef[f, 3 + k : 4 + k, cols] * b
                    rows.append(row)
                pieces.extend(split(jnp.concatenate(rows, axis=0)))
            y = dot(l2[...].astype(bf16), jnp.concatenate(pieces, axis=0))
            for i in range(2):
                at = 2 * i * RP
                yield 2 * pair + i, y[at : at + RP] + y[at + RP : at + 2 * RP]

    @pl.when(coarse)
    def _():
        for f in range(4):
            for j in range(lines):
                place_at(ext, rem, f, j, range(3))
        for t in range(nt):
            cols = slice(t * TILE, (t + 1) * TILE)

            def along(c, axis):
                return sum(
                    metric[3 * axis + b : 3 * axis + b + 1, cols]
                    * grads[c, b * RP : (b + 1) * RP, cols]
                    for b in range(3)
                )

            pq = []
            for f in range(4):
                at = [trs[t, (c * 4 + f) * FP : (c * 4 + f + 1) * FP, :] for c in range(NC)]
                n = [own[f * 8 + i : f * 8 + i + 1, cols] for i in range(4)]
                pq.append(project(at, n) - ext[f, :, cols])
            for c, s in lifted(t, pq):
                k, other = c % 3, 3 - 3 * (c // 3)
                one, two = (k + 1) % 3, (k + 2) % 3
                curl = along(other + two, one) - along(other + one, two)
                vol = curl if c < 3 else -curl
                value = fpad[c * RP : (c + 1) * RP, cols] + STEP * (vol + s)
                out[c, :, cols] = value[:NP]

    @pl.when(fine)
    def _():
        for f in range(4):
            for j in range(lines):
                edge = j < TILE // SUB
                place_at(ext, rem, f, j, range(3) if edge else (2,))
                if edge:
                    place_at(recvn, remn, f, j, range(2))
            base[f] = jnp.where(slots[f : f + 1, :] >= 4 * el, ext[f], 0.0)

        def right_side(t):
            cols = slice(t * TILE, (t + 1) * TILE)
            terms = [
                fpad[c * RP : (c + 1) * RP, cols] - STEP * s
                for c, s in lifted(t, [ext[f, :, cols] for f in range(4)])
            ]
            rhs[t] = stacked(jnp.concatenate(terms, axis=0))

        def edge_blocks(weights, rows):
            z = dot(weights[0], rhs[0])
            for k in range(1, kinds):
                z = jnp.where(kindrow[:, 0:TILE] == k + 1, dot(weights[k], rhs[0]), z)
            zs[0, 0:rows, :] = z

        def inside(row, at, size):
            return jnp.clip(walk[row, at], 0, size - 1)

        def inner_blocks(weights, rows):
            lane = lax.broadcasted_iota(i32, (1, TILE), 1)
            for s in range(steps):
                y = dot(weights[inside(1, s, kinds)], rhs[inside(0, s, nt)])
                if s:
                    here = jnp.logical_and(lane >= walk[2, s], lane < walk[3, s])
                    y = jnp.where(here, y, zs[s, 0:rows, :])
                zs[1 + s, 0:rows, :] = y

        def sweep(no, carry):
            right_side(0)
            edge_blocks(wt, TR)
            fill(0, lambda r: zs[0, r : r + FP, :])
            for i in range(2):
                at = lsl[i : i + 1, :]
                v = jnp.zeros((2 * FP, SUB), f32)
                for h in range(4 * TILE // SUB):
                    f, j = h // (TILE // SUB), h % (TILE // SUB)
                    x = lanes(pq0[f, :, j * SUB : (j + 1) * SUB], at & (SUB - 1))
                    v = jnp.where((at >> (SUB.bit_length() - 1)) == h, x, v)
                sendk[no - 1, i] = v
            copies = later(no)

            @pl.when(fine_prev)
            def _():
                copies[0].start()

            @pl.when(fine_next)
            def _():
                copies[1].start()

            for t in range(1, nt):
                right_side(t)
            inner_blocks(wt, TR)
            for t in range(1, nt):
                last = inside(4, t, steps)
                fill(t, lambda r: zs[1 + last, r : r + FP, :])
            gather(pool, 2 * FP, ext, base)

            @pl.when(fine_prev)
            def _():
                copies[0].wait_send()
                copies[1].wait_recv()
                rem[0] = recvk[no - 1, 0]

            @pl.when(fine_next)
            def _():
                copies[1].wait_send()
                copies[0].wait_recv()
                rem[1] = recvk[no - 1, 1]

            for f in range(4):
                for j in range(TILE // SUB):
                    place_at(ext, rem, f, j, range(2))
            return carry

        lax.fori_loop(1, SWEEPS, sweep, 0)
        for t in range(nt):
            right_side(t)
        edge_blocks(wf, HB)
        inner_blocks(wf, HB)
        for t in range(nt):
            at = 1 + inside(4, t, steps) if t else 0
            cols = slice(t * TILE, (t + 1) * TILE)
            xs[0:HB, cols], xs[HB : 2 * HB, cols] = split(zs[at, 0:HB, :])
        y = dot(xs[0 : 2 * HB, :], pm[...])
        for c in range(NC):
            at = c * RP
            out[c] = y[at : at + NP] + y[HB + at : HB + at + NP]


def shards(*args):
    (fields, metric, scale, angles, nb, send_dom, send_part, kind, deriv, lift, binv) = args
    el = fields.shape[2]
    kinds = binv.shape[0]
    nt, lines = el // TILE, el // SUB
    steps = nt - 1 + kinds - 1
    small, large = constants(el, kinds)
    near = [
        scale, angles, nb, send_dom, send_part.reshape(1, -1), kind.reshape(1, -1), deriv, lift,
        *small,
    ]
    far = [fields, metric, binv, *large]
    vmem, dma = pltpu.VMEM, pltpu.SemaphoreType.DMA
    return pl.pallas_call(
        functools.partial(kernel, el, kinds),
        out_shape=jax.ShapeDtypeStruct(fields.shape, f32),
        in_specs=[pl.BlockSpec(memory_space=vmem)] * len(near)
        + [pl.BlockSpec(memory_space=pl.ANY)] * len(far),
        out_specs=pl.BlockSpec(memory_space=vmem),
        scratch_shapes=[
            *[vmem(a.shape, a.dtype) for a in far],
            vmem((HB, el), f32),
            vmem((32, el), f32),
            vmem((2 * HB + 64, el), bf16),
            vmem((el, 3 * SUB), bf16),
            vmem((8, 3 * SUB), f32),
            vmem((4, el), i32),
            vmem((4, el), f32),
            vmem((1, el), i32),
            vmem(((kinds + 1) * lines, SUB), i32),
            vmem((lines, SUB), i32),
            vmem((el, el), bf16),
            vmem((TILE, 4 * el), bf16),
            vmem((4 * nt * 8, 2 * TILE), bf16),
            vmem((4 * nt * 2 * FP, 2 * TILE), bf16),
            vmem((4, 8, el), f32),
            vmem((4, 8, el), f32),
            vmem((3 * RP, 3 * RP), f32),
            vmem((4 * RP, 16 * FP), f32),
            vmem((nt, TR, TILE), f32),
            vmem((4, 2 * FP, el), f32),
            vmem((4, 2 * FP, el), f32),
            vmem((3, 2 * FP, SUB), f32),
            vmem((3, 8, SUB), f32),
            vmem((kinds, TR, 2 * KB), bf16),
            vmem((kinds, HB, 2 * KB), bf16),
            vmem((nt, 2 * KB, TILE), bf16),
            vmem((1 + steps, TR, TILE), f32),
            vmem((4, 2 * FP, TILE), f32),
            vmem((NC, 3 * RP, el), f32),
            vmem((3, MSG, SUB), f32),
            vmem((3, MSG, SUB), f32),
            vmem((SWEEPS - 1, 2, 2 * FP, SUB), f32),
            vmem((SWEEPS - 1, 2, 2 * FP, SUB), f32),
            pltpu.SMEM((kinds + 1,), i32),
            pltpu.SMEM((5, max(steps, nt)), i32),
            dma((len(far),)), dma((3,)), dma((3,)), dma((SWEEPS - 1, 2)), dma((SWEEPS - 1, 2)),
        ],
        compiler_params=pltpu.CompilerParams(
            collective_id=0, has_side_effects=True, vmem_limit_bytes=56 * 2**20
        ),
    )(*near, *far)


def solution(mesh):
    both = ("group", "dom")
    in_specs = (
        P(None, None, both), P(None, both), P(None, both), P(None, None, both), P(None, both),
        P(None, both), P(both), P(both), P(), P(), P(),
    )
    return jax.shard_map(
        shards, mesh=mesh, in_specs=in_specs, out_specs=P(None, None, both), check_vma=False
    )
```

time: 39.8 us -> 34 us (0.85)
  Pallas kernels: 37.3 us -> 31.5 us
    pallas_call x1, Pallas kernels: 37.3 us -> 31.5 us  [shards(): pl.pallas_call(functools.partial(kernel, el, kinds), out_shape=jax.ShapeD...]
where the time goes in v1:
time: 34 us; the launch traced here: 33.8 us
  Pallas kernels  31.5 us (93%)
  local copies, waits for them, and re-layouts  2.25 us (7%)
    pallas_call x1, Pallas kernels, shards(): pl.pallas_call(functools.partial(kernel, el, kinds), out_shape=jax.ShapeD...  31.5 us
    unnamed x1, local copies, waits for them, and re-layouts  2.25 us

profile of v1, /device:TPU:23, one launch (start us, length us, event | category | flops | bytes accessed | tf_op | source)
XLA Modules:
  0.0 33.8 jit_solution(6864496876239472696)
XLA Ops:
  0.0 31.5 %shard_map.181 = f32[6,35,1024]{2,1,0:T(8,128)} custom-call(f32[4,1024]{1,0:T(4,128)} %scale.1, f32[2,4,1024]{2,1,0:T(4,128)} %angles.1, s32[4,1024]{1,0:T(4,128)} %nb.1, s32[2,128]{1,0:T(2,128)} %send_dom.1, s32[1,128]{1,0:T(1,128)} %bitcast.3, s32[1,1024]{1,0:T(1,128)} %bitcast.2, f32[3,35,35]{2,1,0:T(8,128)} %deriv.1, f32[35,60]{1,0:T(8,128)} %lift.1, ...), custom_call_target="tpu_custom_call" | custom-call | tf_op jit(solution)/shard_map/pallas_call | solution.py:559
  31.5 2.2 %copy.21 = f32[6,35,1024]{2,1,0:T(8,128)} copy(f32[6,35,1024]{2,1,0:T(8,128)} %shard_map.181) | data formatting | bytes 1720320

commit v2 on v1

--- a/solution.py
+++ b/solution.py
@@ -558,7 +558,7 @@
     vmem, dma = pltpu.VMEM, pltpu.SemaphoreType.DMA
     return pl.pallas_call(
         functools.partial(kernel, el, kinds),
-        out_shape=jax.ShapeDtypeStruct(fields.shape, f32),
+        out_shape=pltpu.VMEM(fields.shape, f32),
         in_specs=[pl.BlockSpec(memory_space=vmem)] * len(near)
         + [pl.BlockSpec(memory_space=pl.ANY)] * len(far),
         out_specs=pl.BlockSpec(memory_space=vmem),

time: 34 us -> 31.7 us (0.932)
  local copies, waits for them, and re-layouts: 2.25 us -> 0.95 us
  Pallas kernels: 31.5 us -> 30.6 us
    unnamed x1, local copies, waits for them, and re-layouts: 2.25 us -> 0.95 us
    pallas_call x1, Pallas kernels: 31.5 us -> 30.6 us  [shards(): pl.pallas_call(functools.partial(kernel, el, kinds), out_shape=pltpu.VMEM...]
where the time goes in v2:
time: 31.7 us; the launch traced here: 31.5 us
  Pallas kernels  30.6 us (97%)
  local copies, waits for them, and re-layouts  0.95 us (3%)
    pallas_call x1, Pallas kernels, shards(): pl.pallas_call(functools.partial(kernel, el, kinds), out_shape=pltpu.VMEM...  30.6 us
    unnamed x1, local copies, waits for them, and re-layouts  0.95 us

profile of v2, /device:TPU:23, one launch (start us, length us, event | category | flops | bytes accessed | tf_op | source)
XLA Modules:
  0.0 31.5 jit_solution(7820569091884597687)
XLA Ops:
  0.0 30.6 %shard_map.181 = f32[6,35,1024]{2,1,0:T(8,128)S(1)} custom-call(f32[4,1024]{1,0:T(4,128)} %scale.1, f32[2,4,1024]{2,1,0:T(4,128)} %angles.1, s32[4,1024]{1,0:T(4,128)} %nb.1, s32[2,128]{1,0:T(2,128)} %send_dom.1, s32[1,128]{1,0:T(1,128)} %bitcast.3, s32[1,1024]{1,0:T(1,128)} %bitcast.2, f32[3,35,35]{2,1,0:T(8,128)} %deriv.1, f32[35,60]{1,0:T(8,128)} %lift.1, ...), custom_call_target="tpu_custom_call" | custom-call | tf_op jit(solution)/shard_map/pallas_call | solution.py:559
  30.6 0.9 %copy.21 = f32[6,35,1024]{2,1,0:T(8,128)} copy(f32[6,35,1024]{2,1,0:T(8,128)S(1)} %shard_map.181) | data formatting | bytes 1720320

commit v3 on v2

--- a/solution.py
+++ b/solution.py
@@ -18,6 +18,7 @@
 TR = NC * 4 * FP
 TILE = 256
 SUB = 128
+DIRECT = 1
 MSG = NC * FP + 8
 f32, bf16, i32 = jnp.float32, jnp.bfloat16, jnp.int32
 
@@ -99,7 +100,7 @@
     out,
     fraw, metric, binv, tracep, trace6, rows6, cols6,
     fpad, own, xs, ohs, lnorm, slots, sgn, kindrow, offs, lsl, pm, sel, pooln, pool, recvn, coef,
-    d3, l2, trs, ext, base, rem, remn, wt, wf, rhs, zs, pq0, grads,
+    d3, l2, trs, ext, base, rem, remn, wt, wf, rhs, zs, pqs, acc, grads,
     send0, recv0, sendk, recvk, off, walk,
     in_sem, ssem0, rsem0, ssemk, rsemk,
 ):
@@ -296,8 +297,22 @@
             total = jnp.where(which == h, y[h * rows : (h + 1) * rows], total)
         return total
 
-    def gather(source, rows, dest, under=None):
-        for f in range(4):
+    def gather_direct(tiles, under, dest):
+        for f in range(4 - DIRECT, 4):
+            for j in range(lines):
+                cols = slice(j * SUB, (j + 1) * SUB)
+                at = slots[f : f + 1, cols]
+                total = jnp.zeros((2 * FP, SUB), f32) if under is None else under[f, :, cols]
+                for t in tiles:
+                    for g in range(4):
+                        for i in range(TILE // SUB):
+                            h = g * lines + t * (TILE // SUB) + i
+                            x = lanes(pqs[t, g, :, i * SUB : (i + 1) * SUB], at & (SUB - 1))
+                            total = jnp.where((at >> (SUB.bit_length() - 1)) == h, x, total)
+                dest[f, :, cols] = total
+
+    def gather(source, rows, dest, under=None, faces=4):
+        for f in range(faces):
             s = sel[:, f * el : (f + 1) * el]
             y = dot(source[...], jnp.concatenate([s, s], axis=0))
             dest[f] = pick(y, f, rows, jnp.zeros((rows, el), f32) if under is None else under[f])
@@ -321,8 +336,7 @@
             h = f * nt + t
             pool[h * 2 * FP : (h + 1) * 2 * FP, 0:TILE] = hi
             pool[h * 2 * FP : (h + 1) * 2 * FP, TILE : 2 * TILE] = lo
-            if t == 0:
-                pq0[f] = pq
+            pqs[t, f] = pq
 
     down = lax.broadcasted_iota(i32, (TILE, el), 0)
     for f in range(4):
@@ -343,7 +357,8 @@
         z = dot(tracep[...], stacked(fpad[:, t * TILE : (t + 1) * TILE]))
         trs[t] = z
         fill(t, lambda r: z[r : r + FP])
-    gather(pool, 2 * FP, ext)
+    gather_direct(range(nt), None, ext)
+    gather(pool, 2 * FP, ext, None, 4 - DIRECT)
 
     l2[...] = jnp.zeros_like(l2)
     hi, lo = split(lift[...])
@@ -490,7 +505,7 @@
                 v = jnp.zeros((2 * FP, SUB), f32)
                 for h in range(4 * TILE // SUB):
                     f, j = h // (TILE // SUB), h % (TILE // SUB)
-                    x = lanes(pq0[f, :, j * SUB : (j + 1) * SUB], at & (SUB - 1))
+                    x = lanes(pqs[0, f, :, j * SUB : (j + 1) * SUB], at & (SUB - 1))
                     v = jnp.where((at >> (SUB.bit_length() - 1)) == h, x, v)
                 sendk[no - 1, i] = v
             copies = later(no)
@@ -509,7 +524,8 @@
             for t in range(1, nt):
                 last = inside(4, t, steps)
                 fill(t, lambda r: zs[1 + last, r : r + FP, :])
-            gather(pool, 2 * FP, ext, base)
+            gather_direct(range(nt), base, ext)
+            gather(pool, 2 * FP, ext, base, 4 - DIRECT)
 
             @pl.when(fine_prev)
             def _():
@@ -591,7 +607,8 @@
             vmem((kinds, HB, 2 * KB), bf16),
             vmem((nt, 2 * KB, TILE), bf16),
             vmem((1 + steps, TR, TILE), f32),
-            vmem((4, 2 * FP, TILE), f32),
+            vmem((nt, 4, 2 * FP, TILE), f32),
+            vmem((4, 2 * FP, el), f32),
             vmem((NC, 3 * RP, el), f32),
             vmem((3, MSG, SUB), f32),
             vmem((3, MSG, SUB), f32),

time: 31.7 us -> 30 us (0.946)
  Pallas kernels: 30.6 us -> 28.8 us
    pallas_call x1, Pallas kernels: 30.6 us -> 28.8 us  [shards(): pl.pallas_call(functools.partial(kernel, el, kinds), out_shape=pltpu.VMEM...]
where the time goes in v3:
time: 30 us; the launch traced here: 29.8 us
  Pallas kernels  28.8 us (96%)
  local copies, waits for them, and re-layouts  0.95 us (3%)
    pallas_call x1, Pallas kernels, shards(): pl.pallas_call(functools.partial(kernel, el, kinds), out_shape=pltpu.VMEM...  28.8 us
    unnamed x1, local copies, waits for them, and re-layouts  0.95 us

profile of v3, /device:TPU:23, one launch (start us, length us, event | category | flops | bytes accessed | tf_op | source)
XLA Modules:
  0.0 29.8 jit_solution(2079274970532788250)
XLA Ops:
  0.0 28.8 %shard_map.181 = f32[6,35,1024]{2,1,0:T(8,128)S(1)} custom-call(f32[4,1024]{1,0:T(4,128)} %scale.1, f32[2,4,1024]{2,1,0:T(4,128)} %angles.1, s32[4,1024]{1,0:T(4,128)} %nb.1, s32[2,128]{1,0:T(2,128)} %send_dom.1, s32[1,128]{1,0:T(1,128)} %bitcast.3, s32[1,1024]{1,0:T(1,128)} %bitcast.2, f32[3,35,35]{2,1,0:T(8,128)} %deriv.1, f32[35,60]{1,0:T(8,128)} %lift.1, ...), custom_call_target="tpu_custom_call" | custom-call | tf_op jit(solution)/shard_map/pallas_call | solution.py:575
  28.9 0.9 %copy.21 = f32[6,35,1024]{2,1,0:T(8,128)} copy(f32[6,35,1024]{2,1,0:T(8,128)S(1)} %shard_map.181) | data formatting | bytes 1720320

commit v4 on v3

--- a/solution.py
+++ b/solution.py
@@ -19,6 +19,7 @@
 TILE = 256
 SUB = 128
 DIRECT = 1
+SWAPPED = 2
 MSG = NC * FP + 8
 f32, bf16, i32 = jnp.float32, jnp.bfloat16, jnp.int32
 
@@ -100,7 +101,7 @@
     out,
     fraw, metric, binv, tracep, trace6, rows6, cols6,
     fpad, own, xs, ohs, lnorm, slots, sgn, kindrow, offs, lsl, pm, sel, pooln, pool, recvn, coef,
-    d3, l2, trs, ext, base, rem, remn, wt, wf, rhs, zs, pqs, acc, grads,
+    d3, l2, trs, ext, base, rem, remn, wt, wf, rhs, zs, pqs, rank, last, grads,
     send0, recv0, sendk, recvk, off, walk,
     in_sem, ssem0, rsem0, ssemk, rsemk,
 ):
@@ -169,51 +170,6 @@
     lists = jnp.concatenate([send_dom[0:1, :], send_dom[1:2, :], send_part[...]], axis=1)
     down = lax.broadcasted_iota(i32, (el, 3 * SUB), 0)
     ohs[...] = jnp.where(down == (lists & (el - 1)), 1.0, 0.0).astype(bf16)
-    xs[2 * HB : 2 * HB + 32, :], xs[2 * HB + 32 : 2 * HB + 64, :] = split(own[...])
-
-    loads[0].wait()
-    for c in range(NC):
-        fpad[c * RP + 32 : (c + 1) * RP, :] = jnp.zeros((8, el), f32)
-        fpad[c * RP : c * RP + NP, :] = fraw[c]
-    xs[0:HB, :], xs[HB : 2 * HB, :] = split(fpad[...])
-    loads[1].wait()
-    y = dot(xs[...], ohs[...])
-    at_list = y[2 * HB : 2 * HB + 32] + y[2 * HB + 32 : 2 * HB + 64]
-    face = lists >> shift
-    mine = at_list[0:8]
-    for f in range(1, 4):
-        mine = jnp.where(face == f, at_list[f * 8 : (f + 1) * 8], mine)
-    lnorm[...] = mine
-    t = dot(tracep[...], stacked(y[0:HB] + y[HB : 2 * HB]))
-    for c in range(NC):
-        v = t[c * 4 * FP : c * 4 * FP + FP]
-        for f in range(1, 4):
-            v = jnp.where(face == f, t[(c * 4 + f) * FP : (c * 4 + f + 1) * FP], v)
-        for i in range(3):
-            send0[i, c * FP : (c + 1) * FP, :] = v[:, i * SUB : (i + 1) * SUB]
-    for i in range(3):
-        send0[i, NC * FP : MSG, :] = mine[:, i * SUB : (i + 1) * SUB]
-
-    pl.semaphore_wait(barrier, 1 + has_prev.astype(i32) + has_next.astype(i32))
-
-    @pl.when(has_prev)
-    def _():
-        first[0].start()
-
-    @pl.when(has_next)
-    def _():
-        first[1].start()
-
-    first[2].start()
-
-    @pl.when(coarse)
-    def _():
-        for f in range(4):
-            row = nb[f : f + 1, :]
-            lane = lax.broadcasted_iota(i32, (1, el), 1)
-            slots[f : f + 1, :] = jnp.where(row < 0, lane + f * el, row)
-            sgn[f : f + 1, :] = jnp.where(row < 0, -1.0, 1.0)
-
     @pl.when(fine)
     def _():
         def square(row):
@@ -274,10 +230,71 @@
         lsl[...] = (mine >> shift) * TILE + lookup(mine & (el - 1))
 
         row = line(place)
+        rank[...] = row
         for i in range(nt):
             down = lax.broadcasted_iota(i32, (TILE, el), 0) + i * TILE
             pm[i * TILE : (i + 1) * TILE, :] = jnp.where(down == row, 1.0, 0.0).astype(bf16)
-        xs[2 * HB : 2 * HB + 32, :], xs[2 * HB + 32 : 2 * HB + 64, :] = split(own[...])
+
+    xs[2 * HB : 2 * HB + 32, :], xs[2 * HB + 32 : 2 * HB + 64, :] = split(own[...])
+
+    loads[0].wait()
+    for c in range(NC):
+        fpad[c * RP + 32 : (c + 1) * RP, :] = jnp.zeros((8, el), f32)
+        fpad[c * RP : c * RP + NP, :] = fraw[c]
+    xs[0:HB, :], xs[HB : 2 * HB, :] = split(fpad[...])
+    loads[1].wait()
+    y = dot(xs[...], ohs[...])
+    at_list = y[2 * HB : 2 * HB + 32] + y[2 * HB + 32 : 2 * HB + 64]
+    face = lists >> shift
+    mine = at_list[0:8]
+    for f in range(1, 4):
+        mine = jnp.where(face == f, at_list[f * 8 : (f + 1) * 8], mine)
+    lnorm[...] = mine
+    t = dot(tracep[...], stacked(y[0:HB] + y[HB : 2 * HB]))
+    for c in range(NC):
+        v = t[c * 4 * FP : c * 4 * FP + FP]
+        for f in range(1, 4):
+            v = jnp.where(face == f, t[(c * 4 + f) * FP : (c * 4 + f + 1) * FP], v)
+        for i in range(3):
+            send0[i, c * FP : (c + 1) * FP, :] = v[:, i * SUB : (i + 1) * SUB]
+    for i in range(3):
+        send0[i, NC * FP : MSG, :] = mine[:, i * SUB : (i + 1) * SUB]
+
+    for load in loads[2:]:
+        load.wait()
+
+    @pl.when(fine)
+    def _():
+        for k in range(kinds):
+            b2 = dot(binv[k], cols6[...]).astype(bf16)
+            a = dot(trace6[...], b2).astype(bf16)
+            b = dot(rows6[...], b2).astype(bf16)
+            for i in range(2):
+                wt[k, :, i * KB : (i + 1) * KB] = a
+                wf[k, :, i * KB : (i + 1) * KB] = b
+
+    pl.semaphore_wait(barrier, 1 + has_prev.astype(i32) + has_next.astype(i32))
+
+    @pl.when(has_prev)
+    def _():
+        first[0].start()
+
+    @pl.when(has_next)
+    def _():
+        first[1].start()
+
+    first[2].start()
+
+    @pl.when(coarse)
+    def _():
+        for f in range(4):
+            row = nb[f : f + 1, :]
+            lane = lax.broadcasted_iota(i32, (1, el), 1)
+            slots[f : f + 1, :] = jnp.where(row < 0, lane + f * el, row)
+            sgn[f : f + 1, :] = jnp.where(row < 0, -1.0, 1.0)
+
+    @pl.when(fine)
+    def _():
         y = lax.dot_general(
             xs[...], pm[...], (((1,), (1,)), ((), ())), preferred_element_type=f32
         )
@@ -364,19 +381,6 @@
     hi, lo = split(lift[...])
     for i in range(4):
         l2[i * RP : i * RP + NP, :] = dot(lo if i % 2 else hi, lift_spread[i])
-    for load in loads[2:]:
-        load.wait()
-
-    @pl.when(fine)
-    def _():
-        for k in range(kinds):
-            b2 = dot(binv[k], cols6[...]).astype(bf16)
-            a = dot(trace6[...], b2).astype(bf16)
-            b = dot(rows6[...], b2).astype(bf16)
-            for i in range(2):
-                wt[k, :, i * KB : (i + 1) * KB] = a
-                wf[k, :, i * KB : (i + 1) * KB] = b
-
     @pl.when(coarse)
     def _():
         d3[...] = jnp.zeros_like(d3)
@@ -499,6 +503,8 @@
         def sweep(no, carry):
             right_side(0)
             edge_blocks(wt, TR)
+            for t in range(1, nt):
+                right_side(t)
             fill(0, lambda r: zs[0, r : r + FP, :])
             for i in range(2):
                 at = lsl[i : i + 1, :]
@@ -518,12 +524,10 @@
             def _():
                 copies[1].start()
 
-            for t in range(1, nt):
-                right_side(t)
             inner_blocks(wt, TR)
             for t in range(1, nt):
-                last = inside(4, t, steps)
-                fill(t, lambda r: zs[1 + last, r : r + FP, :])
+                end = inside(4, t, steps)
+                fill(t, lambda r: zs[1 + end, r : r + FP, :])
             gather_direct(range(nt), base, ext)
             gather(pool, 2 * FP, ext, base, 4 - DIRECT)
 
@@ -549,14 +553,26 @@
             right_side(t)
         edge_blocks(wf, HB)
         inner_blocks(wf, HB)
+        part = NC - SWAPPED
         for t in range(nt):
             at = 1 + inside(4, t, steps) if t else 0
             cols = slice(t * TILE, (t + 1) * TILE)
-            xs[0:HB, cols], xs[HB : 2 * HB, cols] = split(zs[at, 0:HB, :])
-        y = dot(xs[0 : 2 * HB, :], pm[...])
-        for c in range(NC):
+            z = zs[at, 0:HB, :]
+            xs[0 : part * RP, cols], xs[HB : HB + part * RP, cols] = split(z[: part * RP])
+            last[:, cols] = z[part * RP :]
+        for j in range(lines):
+            at = rank[:, j * SUB : (j + 1) * SUB]
+            total = jnp.zeros((SWAPPED * RP, SUB), f32)
+            for h in range(lines):
+                x = lanes(last[:, h * SUB : (h + 1) * SUB], at & (SUB - 1))
+                total = jnp.where((at >> (SUB.bit_length() - 1)) == h, x, total)
+            for c in range(SWAPPED):
+                out[part + c, :, j * SUB : (j + 1) * SUB] = total[c * RP : c * RP + NP]
+        x = jnp.concatenate([xs[0 : part * RP, :], xs[HB : HB + part * RP, :]], axis=0)
+        y = dot(x, pm[...])
+        for c in range(part):
             at = c * RP
-            out[c] = y[at : at + NP] + y[HB + at : HB + at + NP]
+            out[c] = y[at : at + NP] + y[part * RP + at : part * RP + at + NP]
 
 
 def shards(*args):
@@ -608,7 +624,8 @@
             vmem((nt, 2 * KB, TILE), bf16),
             vmem((1 + steps, TR, TILE), f32),
             vmem((nt, 4, 2 * FP, TILE), f32),
-            vmem((4, 2 * FP, el), f32),
+            vmem((1, el), i32),
+            vmem((SWAPPED * RP, el), f32),
             vmem((NC, 3 * RP, el), f32),
             vmem((3, MSG, SUB), f32),
             vmem((3, MSG, SUB), f32),

time: 30 us -> 29 us (0.967)
  Pallas kernels: 28.8 us -> 27.8 us
    pallas_call x1, Pallas kernels: 28.8 us -> 27.8 us  [shards(): pl.pallas_call(functools.partial(kernel, el, kinds), out_shape=pltpu.VMEM...]
where the time goes in v4:
time: 29 us; the launch traced here: 28.8 us
  Pallas kernels  27.8 us (96%)
  local copies, waits for them, and re-layouts  0.95 us (3%)
    pallas_call x1, Pallas kernels, shards(): pl.pallas_call(functools.partial(kernel, el, kinds), out_shape=pltpu.VMEM...  27.8 us
    unnamed x1, local copies, waits for them, and re-layouts  0.95 us

profile of v4, /device:TPU:23, one launch (start us, length us, event | category | flops | bytes accessed | tf_op | source)
XLA Modules:
  0.0 28.8 jit_solution(4806436943450459518)
XLA Ops:
  0.0 27.8 %shard_map.181 = f32[6,35,1024]{2,1,0:T(8,128)S(1)} custom-call(f32[4,1024]{1,0:T(4,128)} %scale.1, f32[2,4,1024]{2,1,0:T(4,128)} %angles.1, s32[4,1024]{1,0:T(4,128)} %nb.1, s32[2,128]{1,0:T(2,128)} %send_dom.1, s32[1,128]{1,0:T(1,128)} %bitcast.3, s32[1,1024]{1,0:T(1,128)} %bitcast.2, f32[3,35,35]{2,1,0:T(8,128)} %deriv.1, f32[35,60]{1,0:T(8,128)} %lift.1, ...), custom_call_target="tpu_custom_call" | custom-call | tf_op jit(solution)/shard_map/pallas_call | solution.py:591
  27.9 0.9 %copy.21 = f32[6,35,1024]{2,1,0:T(8,128)} copy(f32[6,35,1024]{2,1,0:T(8,128)S(1)} %shard_map.181) | data formatting | bytes 1720320

commit v5 on v4

--- a/solution.py
+++ b/solution.py
@@ -19,6 +19,7 @@
 TILE = 256
 SUB = 128
 DIRECT = 1
+EXTRA = 2
 SWAPPED = 2
 MSG = NC * FP + 8
 f32, bf16, i32 = jnp.float32, jnp.bfloat16, jnp.int32
@@ -100,7 +101,7 @@
     fields_h, metric_h, binv_h, tracep_h, trace6_h, rows6_h, cols6_h,
     out,
     fraw, metric, binv, tracep, trace6, rows6, cols6,
-    fpad, own, xs, ohs, lnorm, slots, sgn, kindrow, offs, lsl, pm, sel, pooln, pool, recvn, coef,
+    fpad, own, xs, lnorm, slots, sgn, kindrow, offs, lsl, pm, sel, pooln, pool, recvn, coef,
     d3, l2, trs, ext, base, rem, remn, wt, wf, rhs, zs, pqs, rank, last, grads,
     send0, recv0, sendk, recvk, off, walk,
     in_sem, ssem0, rsem0, ssemk, rsemk,
@@ -168,8 +169,6 @@
             own[f * 8 + i : f * 8 + i + 1, :] = parts[i][f : f + 1, :]
         own[f * 8 + 4 : f * 8 + 5, :] = 0.5 * scale[f : f + 1, :]
     lists = jnp.concatenate([send_dom[0:1, :], send_dom[1:2, :], send_part[...]], axis=1)
-    down = lax.broadcasted_iota(i32, (el, 3 * SUB), 0)
-    ohs[...] = jnp.where(down == (lists & (el - 1)), 1.0, 0.0).astype(bf16)
     @pl.when(fine)
     def _():
         def square(row):
@@ -235,22 +234,38 @@
             down = lax.broadcasted_iota(i32, (TILE, el), 0) + i * TILE
             pm[i * TILE : (i + 1) * TILE, :] = jnp.where(down == row, 1.0, 0.0).astype(bf16)
 
-    xs[2 * HB : 2 * HB + 32, :], xs[2 * HB + 32 : 2 * HB + 64, :] = split(own[...])
-
     loads[0].wait()
     for c in range(NC):
         fpad[c * RP + 32 : (c + 1) * RP, :] = jnp.zeros((8, el), f32)
         fpad[c * RP : c * RP + NP, :] = fraw[c]
-    xs[0:HB, :], xs[HB : 2 * HB, :] = split(fpad[...])
-    loads[1].wait()
-    y = dot(xs[...], ohs[...])
-    at_list = y[2 * HB : 2 * HB + 32] + y[2 * HB + 32 : 2 * HB + 64]
+    for load in loads[1:]:
+        load.wait()
+
+    def listed(source):
+        parts = []
+        for i in range(3):
+            at = lists[:, i * SUB : (i + 1) * SUB] & (el - 1)
+            v = jnp.zeros((source.shape[0], SUB), f32)
+            for h in range(lines):
+                x = lanes(source[:, h * SUB : (h + 1) * SUB], at & (SUB - 1))
+                v = jnp.where((at >> (SUB.bit_length() - 1)) == h, x, v)
+            parts.append(v)
+        return jnp.concatenate(parts, axis=1)
+
+    at_list = listed(own)
+    for k in range(kinds):
+        b2 = dot(binv[k], cols6[...]).astype(bf16)
+        a = dot(trace6[...], b2).astype(bf16)
+        b = dot(rows6[...], b2).astype(bf16)
+        for i in range(2):
+            wt[k, :, i * KB : (i + 1) * KB] = a
+            wf[k, :, i * KB : (i + 1) * KB] = b
     face = lists >> shift
     mine = at_list[0:8]
     for f in range(1, 4):
         mine = jnp.where(face == f, at_list[f * 8 : (f + 1) * 8], mine)
     lnorm[...] = mine
-    t = dot(tracep[...], stacked(y[0:HB] + y[HB : 2 * HB]))
+    t = dot(tracep[...], stacked(listed(fpad)))
     for c in range(NC):
         v = t[c * 4 * FP : c * 4 * FP + FP]
         for f in range(1, 4):
@@ -260,19 +275,6 @@
     for i in range(3):
         send0[i, NC * FP : MSG, :] = mine[:, i * SUB : (i + 1) * SUB]
 
-    for load in loads[2:]:
-        load.wait()
-
-    @pl.when(fine)
-    def _():
-        for k in range(kinds):
-            b2 = dot(binv[k], cols6[...]).astype(bf16)
-            a = dot(trace6[...], b2).astype(bf16)
-            b = dot(rows6[...], b2).astype(bf16)
-            for i in range(2):
-                wt[k, :, i * KB : (i + 1) * KB] = a
-                wf[k, :, i * KB : (i + 1) * KB] = b
-
     pl.semaphore_wait(barrier, 1 + has_prev.astype(i32) + has_next.astype(i32))
 
     @pl.when(has_prev)
@@ -295,6 +297,8 @@
 
     @pl.when(fine)
     def _():
+        xs[0:HB, :], xs[HB : 2 * HB, :] = split(fpad[...])
+        xs[2 * HB : 2 * HB + 32, :], xs[2 * HB + 32 : 2 * HB + 64, :] = split(own[...])
         y = lax.dot_general(
             xs[...], pm[...], (((1,), (1,)), ((), ())), preferred_element_type=f32
         )
@@ -309,14 +313,14 @@
                 kindrow[...] = flag >> 1
 
     def pick(y, f, rows, total):
-        which = slots[f : f + 1, :] >> (TILE.bit_length() - 1)
+        which = slots[f : f + 1, 0 : total.shape[1]] >> (TILE.bit_length() - 1)
         for h in range(4 * nt):
             total = jnp.where(which == h, y[h * rows : (h + 1) * rows], total)
         return total
 
     def gather_direct(tiles, under, dest):
-        for f in range(4 - DIRECT, 4):
-            for j in range(lines):
+        for f in range(2, 4):
+            for j in range(0 if f == 3 else lines - EXTRA, lines):
                 cols = slice(j * SUB, (j + 1) * SUB)
                 at = slots[f : f + 1, cols]
                 total = jnp.zeros((2 * FP, SUB), f32) if under is None else under[f, :, cols]
@@ -330,9 +334,11 @@
 
     def gather(source, rows, dest, under=None, faces=4):
         for f in range(faces):
-            s = sel[:, f * el : (f + 1) * el]
+            n = el - EXTRA * SUB if f == 2 and faces < 4 else el
+            s = sel[:, f * el : f * el + n]
             y = dot(source[...], jnp.concatenate([s, s], axis=0))
-            dest[f] = pick(y, f, rows, jnp.zeros((rows, el), f32) if under is None else under[f])
+            total = jnp.zeros((rows, n), f32) if under is None else under[f, :, 0:n]
+            dest[f, :, 0:n] = pick(y, f, rows, total)
 
     def place_at(dest, source, f, j, sources):
         s = slots[f : f + 1, j * SUB : (j + 1) * SUB]
@@ -369,7 +375,17 @@
         sa, ca, sb, cb, w = (own[f * 8 + i : f * 8 + i + 1, :] for i in range(5))
         for i, row in enumerate((w * ca * cb, w * ca * sb, -w * sa, -w * sb, w * cb)):
             coef[f, i : i + 1, :] = row
-    gather(pooln, 8, recvn)
+    gather(pooln, 8, recvn, None, 2)
+    for f in range(2, 4):
+        for j in range(lines):
+            cols = slice(j * SUB, (j + 1) * SUB)
+            at = slots[f : f + 1, cols]
+            total = jnp.zeros((8, SUB), f32)
+            for h in range(4 * lines):
+                g, i = h // lines, h % lines
+                x = lanes(own[g * 8 : g * 8 + 8, i * SUB : (i + 1) * SUB], at & (SUB - 1))
+                total = jnp.where((at >> (SUB.bit_length() - 1)) == h, x, total)
+            recvn[f, :, cols] = total
     for t in range(nt):
         z = dot(tracep[...], stacked(fpad[:, t * TILE : (t + 1) * TILE]))
         trs[t] = z
@@ -599,7 +615,6 @@
             vmem((HB, el), f32),
             vmem((32, el), f32),
             vmem((2 * HB + 64, el), bf16),
-            vmem((el, 3 * SUB), bf16),
             vmem((8, 3 * SUB), f32),
             vmem((4, el), i32),
             vmem((4, el), f32),

time: 29 us -> 27.4 us (0.945)
  Pallas kernels: 27.8 us -> 26.3 us
    pallas_call x1, Pallas kernels: 27.8 us -> 26.3 us  [shards(): pl.pallas_call(functools.partial(kernel, el, kinds), out_shape=pltpu.VMEM...]
where the time goes in v5:
time: 27.4 us; the launch traced here: 27.2 us
  Pallas kernels  26.3 us (96%)
  local copies, waits for them, and re-layouts  0.95 us (3%)
    pallas_call x1, Pallas kernels, shards(): pl.pallas_call(functools.partial(kernel, el, kinds), out_shape=pltpu.VMEM...  26.3 us
    unnamed x1, local copies, waits for them, and re-layouts  0.95 us

profile of v5, /device:TPU:23, one launch (start us, length us, event | category | flops | bytes accessed | tf_op | source)
XLA Modules:
  0.0 27.2 jit_solution(10627197386944453480)
XLA Ops:
  0.0 26.3 %shard_map.181 = f32[6,35,1024]{2,1,0:T(8,128)S(1)} custom-call(f32[4,1024]{1,0:T(4,128)} %scale.1, f32[2,4,1024]{2,1,0:T(4,128)} %angles.1, s32[4,1024]{1,0:T(4,128)} %nb.1, s32[2,128]{1,0:T(2,128)} %send_dom.1, s32[1,128]{1,0:T(1,128)} %bitcast.3, s32[1,1024]{1,0:T(1,128)} %bitcast.2, f32[3,35,35]{2,1,0:T(8,128)} %deriv.1, f32[35,60]{1,0:T(8,128)} %lift.1, ...), custom_call_target="tpu_custom_call" | custom-call | tf_op jit(solution)/shard_map/pallas_call | solution.py:607
  26.3 0.9 %copy.21 = f32[6,35,1024]{2,1,0:T(8,128)} copy(f32[6,35,1024]{2,1,0:T(8,128)S(1)} %shard_map.181) | data formatting | bytes 1720320

commit v6 on v5

--- a/solution.py
+++ b/solution.py
@@ -47,7 +47,7 @@
     rows6 = np.kron(eye6, pad)
     cols6 = np.zeros((NC * NP, KB), np.float32)
     cols6[:, :HB] = rows6.T
-    tracep = np.tile(trace6 @ cols6, (1, 2))
+    tracep = trace6 @ cols6
     spread = np.zeros((2, NP, 3 * RP), np.float32)
     for i in range(NP):
         spread[0, i, i] = spread[0, i, RP + i] = spread[1, i, 2 * RP + i] = 1
@@ -63,7 +63,7 @@
     lines = (kinds + 1) * (el // SUB)
     lower = np.tril(np.ones((lines, lines)), -1)
     small = [jnp.asarray(a, bf16) for a in (upper, lower, spread, lift_spread)]
-    large = [jnp.asarray(a, bf16) for a in (tracep, trace6, rows6, cols6)]
+    large = [jnp.asarray(a, bf16) for a in (tracep, rows6, cols6)]
     return small, large
 
 
@@ -98,10 +98,10 @@
 def kernel(
     el, kinds, scale, angles, nb, send_dom, send_part, kind, deriv, lift,
     upper, lower, spread, lift_spread,
-    fields_h, metric_h, binv_h, tracep_h, trace6_h, rows6_h, cols6_h,
+    fields_h, metric_h, binv_h, tracep_h, rows6_h, cols6_h,
     out,
-    fraw, metric, binv, tracep, trace6, rows6, cols6,
-    fpad, own, xs, lnorm, slots, sgn, kindrow, offs, lsl, pm, sel, pooln, pool, recvn, coef,
+    fraw, metric, binv, tracep, rows6, cols6,
+    fpad, own, xs, lnorm, slots, sgn, kindrow, offs, lsl, pm, sel, pooln, pool, recvn, pc, coef,
     d3, l2, trs, ext, base, rem, remn, wt, wf, rhs, zs, pqs, rank, last, grads,
     send0, recv0, sendk, recvk, off, walk,
     in_sem, ssem0, rsem0, ssemk, rsemk,
@@ -123,7 +123,7 @@
         pltpu.make_async_copy(a, b, in_sem.at[i])
         for i, (a, b) in enumerate((
             (fields_h, fraw), (tracep_h, tracep), (cols6_h, cols6), (binv_h, binv),
-            (trace6_h, trace6), (rows6_h, rows6), (metric_h, metric),
+            (rows6_h, rows6), (metric_h, metric),
         ))
     ]
     for load in loads:
@@ -255,8 +255,8 @@
     at_list = listed(own)
     for k in range(kinds):
         b2 = dot(binv[k], cols6[...]).astype(bf16)
-        a = dot(trace6[...], b2).astype(bf16)
         b = dot(rows6[...], b2).astype(bf16)
+        a = dot(tracep[:, 0:HB], b).astype(bf16)
         for i in range(2):
             wt[k, :, i * KB : (i + 1) * KB] = a
             wf[k, :, i * KB : (i + 1) * KB] = b
@@ -265,7 +265,7 @@
     for f in range(1, 4):
         mine = jnp.where(face == f, at_list[f * 8 : (f + 1) * 8], mine)
     lnorm[...] = mine
-    t = dot(tracep[...], stacked(listed(fpad)))
+    t = dot(jnp.concatenate([tracep[...]] * 2, axis=1), stacked(listed(fpad)))
     for c in range(NC):
         v = t[c * 4 * FP : c * 4 * FP + FP]
         for f in range(1, 4):
@@ -348,13 +348,23 @@
             v = jnp.where(here, lanes(source[i], s & (SUB - 1)), v)
         dest[f, :, j * SUB : (j + 1) * SUB] = v
 
+    def weigh(cols):
+        for f in range(4):
+            sa, ca, sb, cb = (recvn[f, i : i + 1, cols] for i in range(4))
+            sign = sgn[f : f + 1, cols]
+            for i, row in enumerate((ca * cb, ca * sb, sa, cb, sb)):
+                pc[f, i : i + 1, cols] = row
+                pc[f, 8 + i : 9 + i, cols] = sign * row
+
     def fill(t, at_rows):
         cols = slice(t * TILE, (t + 1) * TILE)
         for f in range(4):
             at = [at_rows(c * 4 * FP + f * FP) for c in range(NC)]
-            sign = sgn[f : f + 1, cols]
-            at[:3] = [sign * e for e in at[:3]]
-            pq = project(at, [recvn[f, i : i + 1, cols] for i in range(4)])
+            u, v, sa, cb, sb = (pc[f, i : i + 1, cols] for i in range(5))
+            ue, ve, sae, cbe, sbe = (pc[f, 8 + i : 9 + i, cols] for i in range(5))
+            p = cb * at[4] - sb * at[3] - ue * at[0] - ve * at[1] + sae * at[2]
+            q = sa * at[5] - u * at[3] - v * at[4] - cbe * at[1] + sbe * at[0]
+            pq = jnp.concatenate([p, q], axis=0)
             hi, lo = split(pq)
             h = f * nt + t
             pool[h * 2 * FP : (h + 1) * 2 * FP, 0:TILE] = hi
@@ -375,8 +385,8 @@
         sa, ca, sb, cb, w = (own[f * 8 + i : f * 8 + i + 1, :] for i in range(5))
         for i, row in enumerate((w * ca * cb, w * ca * sb, -w * sa, -w * sb, w * cb)):
             coef[f, i : i + 1, :] = row
-    gather(pooln, 8, recvn, None, 2)
-    for f in range(2, 4):
+    gather(pooln, 8, recvn, None, 1)
+    for f in range(1, 4):
         for j in range(lines):
             cols = slice(j * SUB, (j + 1) * SUB)
             at = slots[f : f + 1, cols]
@@ -386,8 +396,9 @@
                 x = lanes(own[g * 8 : g * 8 + 8, i * SUB : (i + 1) * SUB], at & (SUB - 1))
                 total = jnp.where((at >> (SUB.bit_length() - 1)) == h, x, total)
             recvn[f, :, cols] = total
+    weigh(slice(0, el))
     for t in range(nt):
-        z = dot(tracep[...], stacked(fpad[:, t * TILE : (t + 1) * TILE]))
+        z = dot(jnp.concatenate([tracep[...]] * 2, axis=1), stacked(fpad[:, t * TILE : (t + 1) * TILE]))
         trs[t] = z
         fill(t, lambda r: z[r : r + FP])
     gather_direct(range(nt), None, ext)
@@ -489,6 +500,7 @@
                 if edge:
                     place_at(recvn, remn, f, j, range(2))
             base[f] = jnp.where(slots[f : f + 1, :] >= 4 * el, ext[f], 0.0)
+        weigh(slice(0, TILE))
 
         def right_side(t):
             cols = slice(t * TILE, (t + 1) * TILE)
@@ -626,6 +638,7 @@
             vmem((4 * nt * 8, 2 * TILE), bf16),
             vmem((4 * nt * 2 * FP, 2 * TILE), bf16),
             vmem((4, 8, el), f32),
+            vmem((4, 16, el), f32),
             vmem((4, 8, el), f32),
             vmem((3 * RP, 3 * RP), f32),
             vmem((4 * RP, 16 * FP), f32),

time: 27.4 us -> 27.1 us (0.989)
  Pallas kernels: 26.3 us -> 25.9 us
    pallas_call x1, Pallas kernels: 26.3 us -> 25.9 us  [shards(): pl.pallas_call(functools.partial(kernel, el, kinds), out_shape=pltpu.VMEM...]
where the time goes in v6:
time: 27.1 us; the launch traced here: 26.9 us
  Pallas kernels  25.9 us (96%)
  local copies, waits for them, and re-layouts  0.95 us (4%)
    pallas_call x1, Pallas kernels, shards(): pl.pallas_call(functools.partial(kernel, el, kinds), out_shape=pltpu.VMEM...  25.9 us
    unnamed x1, local copies, waits for them, and re-layouts  0.95 us

profile of v6, /device:TPU:23, one launch (start us, length us, event | category | flops | bytes accessed | tf_op | source)
XLA Modules:
  0.0 26.9 jit_solution(12806677697026973922)
XLA Ops:
  0.0 25.9 %shard_map.172 = f32[6,35,1024]{2,1,0:T(8,128)S(1)} custom-call(f32[4,1024]{1,0:T(4,128)} %scale.1, f32[2,4,1024]{2,1,0:T(4,128)} %angles.1, s32[4,1024]{1,0:T(4,128)} %nb.1, s32[2,128]{1,0:T(2,128)} %send_dom.1, s32[1,128]{1,0:T(1,128)} %bitcast.3, s32[1,1024]{1,0:T(1,128)} %bitcast.2, f32[3,35,35]{2,1,0:T(8,128)} %deriv.1, f32[35,60]{1,0:T(8,128)} %lift.1, ...), custom_call_target="tpu_custom_call" | custom-call | tf_op jit(solution)/shard_map/pallas_call | solution.py:619
  26.0 0.9 %copy.20 = f32[6,35,1024]{2,1,0:T(8,128)} copy(f32[6,35,1024]{2,1,0:T(8,128)S(1)} %shard_map.172) | data formatting | bytes 1720320

commit v7 on v6

--- a/solution.py
+++ b/solution.py
@@ -19,7 +19,7 @@
 TILE = 256
 SUB = 128
 DIRECT = 1
-EXTRA = 2
+EXTRA = 3
 SWAPPED = 2
 MSG = NC * FP + 8
 f32, bf16, i32 = jnp.float32, jnp.bfloat16, jnp.int32
@@ -401,8 +401,8 @@
         z = dot(jnp.concatenate([tracep[...]] * 2, axis=1), stacked(fpad[:, t * TILE : (t + 1) * TILE]))
         trs[t] = z
         fill(t, lambda r: z[r : r + FP])
+    gather(pool, 2 * FP, ext, None, 4 - DIRECT)
     gather_direct(range(nt), None, ext)
-    gather(pool, 2 * FP, ext, None, 4 - DIRECT)
 
     l2[...] = jnp.zeros_like(l2)
     hi, lo = split(lift[...])
@@ -556,8 +556,8 @@
             for t in range(1, nt):
                 end = inside(4, t, steps)
                 fill(t, lambda r: zs[1 + end, r : r + FP, :])
+            gather(pool, 2 * FP, ext, base, 4 - DIRECT)
             gather_direct(range(nt), base, ext)
-            gather(pool, 2 * FP, ext, base, 4 - DIRECT)
 
             @pl.when(fine_prev)
             def _():

time: 27.1 us -> 27 us (level)
  no operation moved by 1% of the time
where the time goes in v7:
time: 27 us; the launch traced here: 26.8 us
  Pallas kernels  25.9 us (96%)
  local copies, waits for them, and re-layouts  0.95 us (4%)
    pallas_call x1, Pallas kernels, shards(): pl.pallas_call(functools.partial(kernel, el, kinds), out_shape=pltpu.VMEM...  25.9 us
    unnamed x1, local copies, waits for them, and re-layouts  0.95 us

profile of v7, /device:TPU:23, one launch (start us, length us, event | category | flops | bytes accessed | tf_op | source)
XLA Modules:
  0.0 26.8 jit_solution(7122059959033874860)
XLA Ops:
  0.0 25.9 %shard_map.172 = f32[6,35,1024]{2,1,0:T(8,128)S(1)} custom-call(f32[4,1024]{1,0:T(4,128)} %scale.1, f32[2,4,1024]{2,1,0:T(4,128)} %angles.1, s32[4,1024]{1,0:T(4,128)} %nb.1, s32[2,128]{1,0:T(2,128)} %send_dom.1, s32[1,128]{1,0:T(1,128)} %bitcast.3, s32[1,1024]{1,0:T(1,128)} %bitcast.2, f32[3,35,35]{2,1,0:T(8,128)} %deriv.1, f32[35,60]{1,0:T(8,128)} %lift.1, ...), custom_call_target="tpu_custom_call" | custom-call | tf_op jit(solution)/shard_map/pallas_call | solution.py:619
  25.9 0.9 %copy.20 = f32[6,35,1024]{2,1,0:T(8,128)} copy(f32[6,35,1024]{2,1,0:T(8,128)S(1)} %shard_map.172) | data formatting | bytes 1720320
